TPU v7x, 32 devices: a whole 2x2x4 slice. The times are simulated.
32 devices in a mesh: groups: 2 (over x), seg: 4 (over z), blk: 4 (over y, core).
Axes of the slice: x: 2, y: 2, z: 4, core: 2. Of those that a mesh axis runs over, the one named last changes fastest.
Arguments:
- base_state: float32 [16, 20, 32, 128], P(('groups', 'seg'), None, 'blk'), parts along dimension 0, may hold values from -6 to 6
- direction: float32 [16, 20, 32, 128], P(('groups', 'seg'), None, 'blk'), parts along dimension 0, may hold values from -6 to 6
- coupling: float32 [40, 20], P('groups'), parts along dimension 0, may hold values from -1.25 to 1.25
- tiles: bfloat16 [8, 32, 16, 128, 128], P('seg', 'blk'), may hold values from -0.15625 to 0.15625
- columns: int32 [8, 32, 16], P('seg', 'blk'), may hold values from 0 to 31, as said below
- wet: int32 [32, 128], P('blk'), may hold values 0 or 1
- basis: float32 [8, 16, 20, 32, 128], P(None, ('groups', 'seg'), None, 'blk'), parts along dimension 1, may hold values from -0.0078125 to 0.0078125
Outputs:
- orthogonal: float32 [16, 20, 32, 128], P(('groups', 'seg'), None, 'blk'), parts along dimension 0
- coefficients: float32 [18], P('groups'), parts along dimension 0
There are 2 independent parts, one for each index of `groups`. A program takes and returns all parts, laid end to end along the dimension named above; an argument that names none is the same for every part. Nothing has to cross between parts.
Inputs may be any that keep to these rules, and one draw needn't show every extreme that they name: columns[s, r, k] = (r + d) mod 32 for some whole d with -2 <= d <= 2; in every segment some entry has d = 2 and some has d = -2.
All inputs are finite; a program needn't handle non-finite values. No bound on the sum of `wet` on one device may be relied on, other than what follows from the above.
Results may differ from a plain program's by a relative error of at most 0.04.
Values may be sent and summed in bfloat16 or wider, within the bound.
A program may use at most 128 MiB of HBM per device.

v0:
```python
import jax
import jax.numpy as jnp
from jax import lax
from jax.sharding import PartitionSpec as P

STEPS = 18


def with_halo(cells, sides, width):
    for axis, dim in sides:
        count = lax.axis_size(axis)
        head = lax.slice_in_dim(cells, 0, width, axis=dim)
        tail = lax.slice_in_dim(cells, cells.shape[dim] - width, cells.shape[dim], axis=dim)
        cells = jnp.concatenate(
            [
                lax.ppermute(tail, axis, [(i, (i + 1) % count) for i in range(count)]),
                cells,
                lax.ppermute(head, axis, [((i + 1) % count, i) for i in range(count)]),
            ],
            axis=dim,
        )
    return cells


def shifted(block, axis, distance):
    devices = range(lax.axis_size(axis))
    route = [((i - distance) % len(devices), i) for i in devices]
    return lax.ppermute(block, axis, route)


def pick_blocks(whole, cols_s):
    return jnp.take(whole, cols_s.reshape(-1), axis=1)


def transport(extended, places, tiles_part):
    seg_here = extended.shape[0]
    tracers = extended.shape[1]
    points = extended.shape[3]
    rows = places.shape[1]
    stored = places.shape[2]
    picked = jax.vmap(pick_blocks)(extended, places)
    picked = picked.reshape(seg_here, tracers, rows, stored, points)
    return jnp.einsum("srkpq,strkq->strp", tiles_part, picked, preferred_element_type=jnp.float32)


def forcing(u, slope, coupling):
    source = jnp.einsum("tu,sunp->stnp", coupling, slope * u, precision=lax.Precision.HIGHEST)
    return (u + 0.5 * source).astype(jnp.bfloat16)


def on_device(base_state, direction, coupling, tiles, columns, wet, basis):
    seg_here = direction.shape[0]
    tracers = direction.shape[1]
    blocks = direction.shape[2]
    points = direction.shape[3]
    reach = max(1, blocks // 4)
    total = blocks * lax.axis_size("blk")
    entries = float(seg_here * lax.axis_size("seg") * tracers * total * points)
    first = lax.axis_index("blk") * blocks
    slope = 1.0 - jnp.tanh(base_state) ** 2
    wetf = wet.astype(jnp.float32)
    near = (columns - first + reach) % total

    def single(index, u):
        drive = forcing(u, slope, coupling)
        extended = with_halo(drive, (("blk", 2),), reach)
        return transport(extended, near, tiles) * wetf

    final = lax.fori_loop(0, STEPS, single, direction)
    after = shifted(direction[0:1], "seg", -1)
    following = jnp.concatenate([direction[1:], after], axis=0)
    shot = final - following
    local_proj = jnp.einsum("jstnp,stnp->j", basis, shot, precision=lax.Precision.HIGHEST)
    proj = lax.psum(local_proj, ("seg", "blk"))
    orthogonal = shot - jnp.einsum("j,jstnp->stnp", proj, basis, precision=lax.Precision.HIGHEST)
    squared = lax.psum(jnp.sum(orthogonal * orthogonal), ("seg", "blk"))
    length = jnp.sqrt(squared / entries)
    return (orthogonal, jnp.concatenate([proj, length[None]]))


def solution(mesh):
    in_specs = (
        P(("groups", "seg"), None, "blk", None),
        P(("groups", "seg"), None, "blk", None),
        P("groups", None),
        P("seg", "blk", None, None, None),
        P("seg", "blk", None),
        P("blk", None),
        P(None, ("groups", "seg"), None, "blk", None),
    )
    out_specs = (P(("groups", "seg"), None, "blk", None), P("groups"))
    return jax.shard_map(
        on_device, mesh=mesh, in_specs=in_specs, out_specs=out_specs, check_vma=False
    )
```

profile of v0, /device:TPU:0, one launch (start us, length us, event | category | flops | bytes accessed | tf_op | source)
XLA Modules:
  0.0 270.3 jit_solution(12659576681942761652)
XLA Ops:
  2.3 5.0 %collective-permute-start.2 = (f32[1,20,8,128]{3,2,1,0:T(8,128)}, f32[1,20,8,128]{3,2,1,0:T(8,128)}, u32[]{:S(2)}, u32[]{:S(2)}) collective-permute-start(f32[1,20,8,128]{3,2,1,0:T(8,128)} %get-tuple-element.66), channel_id=1, source_target_pairs={{4,0},{8,4},{12,8},{0,12},{5,1},{9,5},{13,9},{1,13},{6,2},{10,6},{... | collective-permute-start | bytes 245768 | tf_op jit(solution)/shard_map/ppermute | solution.py:28
  10.8 190.2 %while.11 = (s32[]{:T(128)}, f32[2,20,8,128]{3,1,2,0:T(8,128)S(1)}, s32[2,8,16]{2,1,0:T(8,128)S(1)}, f32[2,20,8,128]{3,1,2,0:T(8,128)S(1)}, f32[20,20]{1,0:T(8,1...) while((s32[]{:T(128)}, f32[2,20,8,128]{3,1,2,0:T(8,128)S(1)}, ...), condition=%wide.wide.region_1.2_spmd, body=%wide.wide.region_0.1_spmd.sunk | while | flops 178589184 | bytes 13397229 | solution.py:69
  17.2 4.7 %fusion.64 = f32[2,20,8,128]{3,1,2,0:T(8,128)S(1)} fusion(bf16[2,8,16,128,128]{4,3,2,1,0:T(8,128)(2,1)} %get-tuple-element.173, bf16[2,20,8,16,128]{4,1,3,2,0:T(8,128)(2,1)S(1)} %bitcast.63, pred[2,8,16]{2,1,0:T(8,128)(4,1)S(1)} %compare_and_fusion.3, f32[8,128]{1,0:T(8,128)S(1)} %get-tuple-element.174), kind=kOutput, calls=%fused_computation.9.clone.clone.1 | convolution fusion | flops 168468480 | bytes 9867520 | tf_op jit(solution)/shard_map/while/body/eval_jaxpr/srkpq,strkq->strp/dot_general | solution.py:43
  27.7 4.7 %fusion.64 = f32[2,20,8,128]{3,1,2,0:T(8,128)S(1)} fusion(bf16[2,8,16,128,128]{4,3,2,1,0:T(8,128)(2,1)} %get-tuple-element.173, bf16[2,20,8,16,128]{4,1,3,2,0:T(8,128)(2,1)S(1)} %bitcast.63, pred[2,8,16]{2,1,0:T(8,128)(4,1)S(1)} %compare_and_fusion.3, f32[8,128]{1,0:T(8,128)S(1)} %get-tuple-element.174), kind=kOutput, calls=%fused_computation.9.clone.clone.1 | convolution fusion | flops 168468480 | bytes 9867520 | tf_op jit(solution)/shard_map/while/body/eval_jaxpr/srkpq,strkq->strp/dot_general | solution.py:43
  38.2 4.7 %fusion.64 = f32[2,20,8,128]{3,1,2,0:T(8,128)S(1)} fusion(bf16[2,8,16,128,128]{4,3,2,1,0:T(8,128)(2,1)} %get-tuple-element.173, bf16[2,20,8,16,128]{4,1,3,2,0:T(8,128)(2,1)S(1)} %bitcast.63, pred[2,8,16]{2,1,0:T(8,128)(4,1)S(1)} %compare_and_fusion.3, f32[8,128]{1,0:T(8,128)S(1)} %get-tuple-element.174), kind=kOutput, calls=%fused_computation.9.clone.clone.1 | convolution fusion | flops 168468480 | bytes 9867520 | tf_op jit(solution)/shard_map/while/body/eval_jaxpr/srkpq,strkq->strp/dot_general | solution.py:43
  48.8 4.7 %fusion.64 = f32[2,20,8,128]{3,1,2,0:T(8,128)S(1)} fusion(bf16[2,8,16,128,128]{4,3,2,1,0:T(8,128)(2,1)} %get-tuple-element.173, bf16[2,20,8,16,128]{4,1,3,2,0:T(8,128)(2,1)S(1)} %bitcast.63, pred[2,8,16]{2,1,0:T(8,128)(4,1)S(1)} %compare_and_fusion.3, f32[8,128]{1,0:T(8,128)S(1)} %get-tuple-element.174), kind=kOutput, calls=%fused_computation.9.clone.clone.1 | convolution fusion | flops 168468480 | bytes 9867520 | tf_op jit(solution)/shard_map/while/body/eval_jaxpr/srkpq,strkq->strp/dot_general | solution.py:43
  59.3 4.7 %fusion.64 = f32[2,20,8,128]{3,1,2,0:T(8,128)S(1)} fusion(bf16[2,8,16,128,128]{4,3,2,1,0:T(8,128)(2,1)} %get-tuple-element.173, bf16[2,20,8,16,128]{4,1,3,2,0:T(8,128)(2,1)S(1)} %bitcast.63, pred[2,8,16]{2,1,0:T(8,128)(4,1)S(1)} %compare_and_fusion.3, f32[8,128]{1,0:T(8,128)S(1)} %get-tuple-element.174), kind=kOutput, calls=%fused_computation.9.clone.clone.1 | convolution fusion | flops 168468480 | bytes 9867520 | tf_op jit(solution)/shard_map/while/body/eval_jaxpr/srkpq,strkq->strp/dot_general | solution.py:43
  69.8 4.7 %fusion.64 = f32[2,20,8,128]{3,1,2,0:T(8,128)S(1)} fusion(bf16[2,8,16,128,128]{4,3,2,1,0:T(8,128)(2,1)} %get-tuple-element.173, bf16[2,20,8,16,128]{4,1,3,2,0:T(8,128)(2,1)S(1)} %bitcast.63, pred[2,8,16]{2,1,0:T(8,128)(4,1)S(1)} %compare_and_fusion.3, f32[8,128]{1,0:T(8,128)S(1)} %get-tuple-element.174), kind=kOutput, calls=%fused_computation.9.clone.clone.1 | convolution fusion | flops 168468480 | bytes 9867520 | tf_op jit(solution)/shard_map/while/body/eval_jaxpr/srkpq,strkq->strp/dot_general | solution.py:43
  80.4 4.7 %fusion.64 = f32[2,20,8,128]{3,1,2,0:T(8,128)S(1)} fusion(bf16[2,8,16,128,128]{4,3,2,1,0:T(8,128)(2,1)} %get-tuple-element.173, bf16[2,20,8,16,128]{4,1,3,2,0:T(8,128)(2,1)S(1)} %bitcast.63, pred[2,8,16]{2,1,0:T(8,128)(4,1)S(1)} %compare_and_fusion.3, f32[8,128]{1,0:T(8,128)S(1)} %get-tuple-element.174), kind=kOutput, calls=%fused_computation.9.clone.clone.1 | convolution fusion | flops 168468480 | bytes 9867520 | tf_op jit(solution)/shard_map/while/body/eval_jaxpr/srkpq,strkq->strp/dot_general | solution.py:43
  90.9 4.7 %fusion.64 = f32[2,20,8,128]{3,1,2,0:T(8,128)S(1)} fusion(bf16[2,8,16,128,128]{4,3,2,1,0:T(8,128)(2,1)} %get-tuple-element.173, bf16[2,20,8,16,128]{4,1,3,2,0:T(8,128)(2,1)S(1)} %bitcast.63, pred[2,8,16]{2,1,0:T(8,128)(4,1)S(1)} %compare_and_fusion.3, f32[8,128]{1,0:T(8,128)S(1)} %get-tuple-element.174), kind=kOutput, calls=%fused_computation.9.clone.clone.1 | convolution fusion | flops 168468480 | bytes 9867520 | tf_op jit(solution)/shard_map/while/body/eval_jaxpr/srkpq,strkq->strp/dot_general | solution.py:43
  101.4 4.7 %fusion.64 = f32[2,20,8,128]{3,1,2,0:T(8,128)S(1)} fusion(bf16[2,8,16,128,128]{4,3,2,1,0:T(8,128)(2,1)} %get-tuple-element.173, bf16[2,20,8,16,128]{4,1,3,2,0:T(8,128)(2,1)S(1)} %bitcast.63, pred[2,8,16]{2,1,0:T(8,128)(4,1)S(1)} %compare_and_fusion.3, f32[8,128]{1,0:T(8,128)S(1)} %get-tuple-element.174), kind=kOutput, calls=%fused_computation.9.clone.clone.1 | convolution fusion | flops 168468480 | bytes 9867520 | tf_op jit(solution)/shard_map/while/body/eval_jaxpr/srkpq,strkq->strp/dot_general | solution.py:43
  112.0 4.7 %fusion.64 = f32[2,20,8,128]{3,1,2,0:T(8,128)S(1)} fusion(bf16[2,8,16,128,128]{4,3,2,1,0:T(8,128)(2,1)} %get-tuple-element.173, bf16[2,20,8,16,128]{4,1,3,2,0:T(8,128)(2,1)S(1)} %bitcast.63, pred[2,8,16]{2,1,0:T(8,128)(4,1)S(1)} %compare_and_fusion.3, f32[8,128]{1,0:T(8,128)S(1)} %get-tuple-element.174), kind=kOutput, calls=%fused_computation.9.clone.clone.1 | convolution fusion | flops 168468480 | bytes 9867520 | tf_op jit(solution)/shard_map/while/body/eval_jaxpr/srkpq,strkq->strp/dot_general | solution.py:43
  122.5 4.7 %fusion.64 = f32[2,20,8,128]{3,1,2,0:T(8,128)S(1)} fusion(bf16[2,8,16,128,128]{4,3,2,1,0:T(8,128)(2,1)} %get-tuple-element.173, bf16[2,20,8,16,128]{4,1,3,2,0:T(8,128)(2,1)S(1)} %bitcast.63, pred[2,8,16]{2,1,0:T(8,128)(4,1)S(1)} %compare_and_fusion.3, f32[8,128]{1,0:T(8,128)S(1)} %get-tuple-element.174), kind=kOutput, calls=%fused_computation.9.clone.clone.1 | convolution fusion | flops 168468480 | bytes 9867520 | tf_op jit(solution)/shard_map/while/body/eval_jaxpr/srkpq,strkq->strp/dot_general | solution.py:43
  133.0 4.7 %fusion.64 = f32[2,20,8,128]{3,1,2,0:T(8,128)S(1)} fusion(bf16[2,8,16,128,128]{4,3,2,1,0:T(8,128)(2,1)} %get-tuple-element.173, bf16[2,20,8,16,128]{4,1,3,2,0:T(8,128)(2,1)S(1)} %bitcast.63, pred[2,8,16]{2,1,0:T(8,128)(4,1)S(1)} %compare_and_fusion.3, f32[8,128]{1,0:T(8,128)S(1)} %get-tuple-element.174), kind=kOutput, calls=%fused_computation.9.clone.clone.1 | convolution fusion | flops 168468480 | bytes 9867520 | tf_op jit(solution)/shard_map/while/body/eval_jaxpr/srkpq,strkq->strp/dot_general | solution.py:43
  143.6 4.7 %fusion.64 = f32[2,20,8,128]{3,1,2,0:T(8,128)S(1)} fusion(bf16[2,8,16,128,128]{4,3,2,1,0:T(8,128)(2,1)} %get-tuple-element.173, bf16[2,20,8,16,128]{4,1,3,2,0:T(8,128)(2,1)S(1)} %bitcast.63, pred[2,8,16]{2,1,0:T(8,128)(4,1)S(1)} %compare_and_fusion.3, f32[8,128]{1,0:T(8,128)S(1)} %get-tuple-element.174), kind=kOutput, calls=%fused_computation.9.clone.clone.1 | convolution fusion | flops 168468480 | bytes 9867520 | tf_op jit(solution)/shard_map/while/body/eval_jaxpr/srkpq,strkq->strp/dot_general | solution.py:43
  154.1 4.7 %fusion.64 = f32[2,20,8,128]{3,1,2,0:T(8,128)S(1)} fusion(bf16[2,8,16,128,128]{4,3,2,1,0:T(8,128)(2,1)} %get-tuple-element.173, bf16[2,20,8,16,128]{4,1,3,2,0:T(8,128)(2,1)S(1)} %bitcast.63, pred[2,8,16]{2,1,0:T(8,128)(4,1)S(1)} %compare_and_fusion.3, f32[8,128]{1,0:T(8,128)S(1)} %get-tuple-element.174), kind=kOutput, calls=%fused_computation.9.clone.clone.1 | convolution fusion | flops 168468480 | bytes 9867520 | tf_op jit(solution)/shard_map/while/body/eval_jaxpr/srkpq,strkq->strp/dot_general | solution.py:43
  164.7 4.7 %fusion.64 = f32[2,20,8,128]{3,1,2,0:T(8,128)S(1)} fusion(bf16[2,8,16,128,128]{4,3,2,1,0:T(8,128)(2,1)} %get-tuple-element.173, bf16[2,20,8,16,128]{4,1,3,2,0:T(8,128)(2,1)S(1)} %bitcast.63, pred[2,8,16]{2,1,0:T(8,128)(4,1)S(1)} %compare_and_fusion.3, f32[8,128]{1,0:T(8,128)S(1)} %get-tuple-element.174), kind=kOutput, calls=%fused_computation.9.clone.clone.1 | convolution fusion | flops 168468480 | bytes 9867520 | tf_op jit(solution)/shard_map/while/body/eval_jaxpr/srkpq,strkq->strp/dot_general | solution.py:43
  175.2 4.7 %fusion.64 = f32[2,20,8,128]{3,1,2,0:T(8,128)S(1)} fusion(bf16[2,8,16,128,128]{4,3,2,1,0:T(8,128)(2,1)} %get-tuple-element.173, bf16[2,20,8,16,128]{4,1,3,2,0:T(8,128)(2,1)S(1)} %bitcast.63, pred[2,8,16]{2,1,0:T(8,128)(4,1)S(1)} %compare_and_fusion.3, f32[8,128]{1,0:T(8,128)S(1)} %get-tuple-element.174), kind=kOutput, calls=%fused_computation.9.clone.clone.1 | convolution fusion | flops 168468480 | bytes 9867520 | tf_op jit(solution)/shard_map/while/body/eval_jaxpr/srkpq,strkq->strp/dot_general | solution.py:43
  185.7 4.7 %fusion.64 = f32[2,20,8,128]{3,1,2,0:T(8,128)S(1)} fusion(bf16[2,8,16,128,128]{4,3,2,1,0:T(8,128)(2,1)} %get-tuple-element.173, bf16[2,20,8,16,128]{4,1,3,2,0:T(8,128)(2,1)S(1)} %bitcast.63, pred[2,8,16]{2,1,0:T(8,128)(4,1)S(1)} %compare_and_fusion.3, f32[8,128]{1,0:T(8,128)S(1)} %get-tuple-element.174), kind=kOutput, calls=%fused_computation.9.clone.clone.1 | convolution fusion | flops 168468480 | bytes 9867520 | tf_op jit(solution)/shard_map/while/body/eval_jaxpr/srkpq,strkq->strp/dot_general | solution.py:43
  196.3 4.7 %fusion.64 = f32[2,20,8,128]{3,1,2,0:T(8,128)S(1)} fusion(bf16[2,8,16,128,128]{4,3,2,1,0:T(8,128)(2,1)} %get-tuple-element.173, bf16[2,20,8,16,128]{4,1,3,2,0:T(8,128)(2,1)S(1)} %bitcast.63, pred[2,8,16]{2,1,0:T(8,128)(4,1)S(1)} %compare_and_fusion.3, f32[8,128]{1,0:T(8,128)S(1)} %get-tuple-element.174), kind=kOutput, calls=%fused_computation.9.clone.clone.1 | convolution fusion | flops 168468480 | bytes 9867520 | tf_op jit(solution)/shard_map/while/body/eval_jaxpr/srkpq,strkq->strp/dot_general | solution.py:43
  202.0 3.4 %fusion.27 = f32[8]{0:T(128)S(1)} fusion(f32[8,2,20,8,128]{4,3,2,1,0:T(8,128)S(1)} %copy-done, f32[2,20,8,128,1]{3,2,1,0,4:T(8,128)S(1)} %fusion.34), kind=kOutput, calls=%fused_computation.27 | convolution fusion | flops 3932160 | bytes 1474592 | tf_op jit(solution)/shard_map/jstnp,stnp->j/dot_general | solution.py:73
  205.4 29.5 %psum.14 = f32[8]{0:T(128)S(1)} all-reduce(f32[8]{0:T(128)S(1)} %fusion.27), channel_id=1, replica_groups=mesh['groups'=2,'seg'=4,'blk'=4] {'seg','blk'}, use_global_device_ids=true, to_apply=%region_2.3 | all-reduce | flops 8 | bytes 64 | tf_op jit(solution)/shard_map/psum | solution.py:74
  236.7 2.2 multiply_reduce_fusion
  238.9 30.1 %psum.15 = f32[]{:T(128)} all-reduce(f32[]{:T(128)} %get-tuple-element.61), channel_id=1, replica_groups=mesh['groups'=2,'seg'=4,'blk'=4] {'seg','blk'}, use_global_device_ids=true, to_apply=%region_4.5 | all-reduce | flops 1 | bytes 8 | tf_op jit(solution)/shard_map/psum | solution.py:76
  (192 shorter events, 112.8 us)
Async XLA Ops:
  2.3 198.7 %collective-permute-start.2 = (f32[1,20,8,128]{3,2,1,0:T(8,128)}, f32[1,20,8,128]{3,2,1,0:T(8,128)}, u32[]{:S(2)}, u32[]{:S(2)}) collective-permute-start(f32[1,20,8,128]{3,2,1,0:T(8,128)} %get-tuple-element.66), channel_id=1, source_target_pairs={{4,0},{8,4},{12,8},{0,12},{5,1},{9,5},{13,9},{1,13},{6,2},{10,6},{... | collective-permute-start | bytes 245768 | tf_op jit(solution)/shard_map/ppermute | solution.py:28
  11.8 2.3 collective-permute-start
  12.6 3.3 %collective-permute-start.1 = (bf16[2,20,2,128]{3,1,2,0:T(8,128)(2,1)S(1)}, bf16[2,20,2,128]{3,1,2,0:T(8,128)(2,1)S(1)}, u32[]{:S(2)}, u32[]{:S(2)}) collective-permute-start(bf16[2,20,2,128]{3,1,2,0:T(8,128)(2,1)S(1)} %get-tuple-element.149), channel_id=1, source_target_pairs={{0,1},{1,2},{2,3},{3,0},{4,5},{5,6},{6,7},{7,4},{8,9},{9,10},{10,1... | collective-permute-start | bytes 61448 | tf_op jit(solution)/shard_map/while/body/eval_jaxpr/ppermute | solution.py:16
  23.0 1.6 collective-permute-start
  23.0 3.3 %collective-permute-start.1 = (bf16[2,20,2,128]{3,1,2,0:T(8,128)(2,1)S(1)}, bf16[2,20,2,128]{3,1,2,0:T(8,128)(2,1)S(1)}, u32[]{:S(2)}, u32[]{:S(2)}) collective-permute-start(bf16[2,20,2,128]{3,1,2,0:T(8,128)(2,1)S(1)} %get-tuple-element.149), channel_id=1, source_target_pairs={{0,1},{1,2},{2,3},{3,0},{4,5},{5,6},{6,7},{7,4},{8,9},{9,10},{10,1... | collective-permute-start | bytes 61448 | tf_op jit(solution)/shard_map/while/body/eval_jaxpr/ppermute | solution.py:16
  33.6 3.3 %collective-permute-start.1 = (bf16[2,20,2,128]{3,1,2,0:T(8,128)(2,1)S(1)}, bf16[2,20,2,128]{3,1,2,0:T(8,128)(2,1)S(1)}, u32[]{:S(2)}, u32[]{:S(2)}) collective-permute-start(bf16[2,20,2,128]{3,1,2,0:T(8,128)(2,1)S(1)} %get-tuple-element.149), channel_id=1, source_target_pairs={{0,1},{1,2},{2,3},{3,0},{4,5},{5,6},{6,7},{7,4},{8,9},{9,10},{10,1... | collective-permute-start | bytes 61448 | tf_op jit(solution)/shard_map/while/body/eval_jaxpr/ppermute | solution.py:16
  44.0 1.6 collective-permute-start
  44.1 3.3 %collective-permute-start.1 = (bf16[2,20,2,128]{3,1,2,0:T(8,128)(2,1)S(1)}, bf16[2,20,2,128]{3,1,2,0:T(8,128)(2,1)S(1)}, u32[]{:S(2)}, u32[]{:S(2)}) collective-permute-start(bf16[2,20,2,128]{3,1,2,0:T(8,128)(2,1)S(1)} %get-tuple-element.149), channel_id=1, source_target_pairs={{0,1},{1,2},{2,3},{3,0},{4,5},{5,6},{6,7},{7,4},{8,9},{9,10},{10,1... | collective-permute-start | bytes 61448 | tf_op jit(solution)/shard_map/while/body/eval_jaxpr/ppermute | solution.py:16
  54.6 1.6 collective-permute-start
  54.6 3.3 %collective-permute-start.1 = (bf16[2,20,2,128]{3,1,2,0:T(8,128)(2,1)S(1)}, bf16[2,20,2,128]{3,1,2,0:T(8,128)(2,1)S(1)}, u32[]{:S(2)}, u32[]{:S(2)}) collective-permute-start(bf16[2,20,2,128]{3,1,2,0:T(8,128)(2,1)S(1)} %get-tuple-element.149), channel_id=1, source_target_pairs={{0,1},{1,2},{2,3},{3,0},{4,5},{5,6},{6,7},{7,4},{8,9},{9,10},{10,1... | collective-permute-start | bytes 61448 | tf_op jit(solution)/shard_map/while/body/eval_jaxpr/ppermute | solution.py:16
  65.2 3.3 %collective-permute-start.1 = (bf16[2,20,2,128]{3,1,2,0:T(8,128)(2,1)S(1)}, bf16[2,20,2,128]{3,1,2,0:T(8,128)(2,1)S(1)}, u32[]{:S(2)}, u32[]{:S(2)}) collective-permute-start(bf16[2,20,2,128]{3,1,2,0:T(8,128)(2,1)S(1)} %get-tuple-element.149), channel_id=1, source_target_pairs={{0,1},{1,2},{2,3},{3,0},{4,5},{5,6},{6,7},{7,4},{8,9},{9,10},{10,1... | collective-permute-start | bytes 61448 | tf_op jit(solution)/shard_map/while/body/eval_jaxpr/ppermute | solution.py:16
  75.7 3.3 %collective-permute-start.1 = (bf16[2,20,2,128]{3,1,2,0:T(8,128)(2,1)S(1)}, bf16[2,20,2,128]{3,1,2,0:T(8,128)(2,1)S(1)}, u32[]{:S(2)}, u32[]{:S(2)}) collective-permute-start(bf16[2,20,2,128]{3,1,2,0:T(8,128)(2,1)S(1)} %get-tuple-element.149), channel_id=1, source_target_pairs={{0,1},{1,2},{2,3},{3,0},{4,5},{5,6},{6,7},{7,4},{8,9},{9,10},{10,1... | collective-permute-start | bytes 61448 | tf_op jit(solution)/shard_map/while/body/eval_jaxpr/ppermute | solution.py:16
  86.2 3.3 %collective-permute-start.1 = (bf16[2,20,2,128]{3,1,2,0:T(8,128)(2,1)S(1)}, bf16[2,20,2,128]{3,1,2,0:T(8,128)(2,1)S(1)}, u32[]{:S(2)}, u32[]{:S(2)}) collective-permute-start(bf16[2,20,2,128]{3,1,2,0:T(8,128)(2,1)S(1)} %get-tuple-element.149), channel_id=1, source_target_pairs={{0,1},{1,2},{2,3},{3,0},{4,5},{5,6},{6,7},{7,4},{8,9},{9,10},{10,1... | collective-permute-start | bytes 61448 | tf_op jit(solution)/shard_map/while/body/eval_jaxpr/ppermute | solution.py:16
  96.8 3.3 %collective-permute-start.1 = (bf16[2,20,2,128]{3,1,2,0:T(8,128)(2,1)S(1)}, bf16[2,20,2,128]{3,1,2,0:T(8,128)(2,1)S(1)}, u32[]{:S(2)}, u32[]{:S(2)}) collective-permute-start(bf16[2,20,2,128]{3,1,2,0:T(8,128)(2,1)S(1)} %get-tuple-element.149), channel_id=1, source_target_pairs={{0,1},{1,2},{2,3},{3,0},{4,5},{5,6},{6,7},{7,4},{8,9},{9,10},{10,1... | collective-permute-start | bytes 61448 | tf_op jit(solution)/shard_map/while/body/eval_jaxpr/ppermute | solution.py:16
  107.2 1.6 collective-permute-start
  107.3 3.3 %collective-permute-start.1 = (bf16[2,20,2,128]{3,1,2,0:T(8,128)(2,1)S(1)}, bf16[2,20,2,128]{3,1,2,0:T(8,128)(2,1)S(1)}, u32[]{:S(2)}, u32[]{:S(2)}) collective-permute-start(bf16[2,20,2,128]{3,1,2,0:T(8,128)(2,1)S(1)} %get-tuple-element.149), channel_id=1, source_target_pairs={{0,1},{1,2},{2,3},{3,0},{4,5},{5,6},{6,7},{7,4},{8,9},{9,10},{10,1... | collective-permute-start | bytes 61448 | tf_op jit(solution)/shard_map/while/body/eval_jaxpr/ppermute | solution.py:16
  117.8 3.3 %collective-permute-start.1 = (bf16[2,20,2,128]{3,1,2,0:T(8,128)(2,1)S(1)}, bf16[2,20,2,128]{3,1,2,0:T(8,128)(2,1)S(1)}, u32[]{:S(2)}, u32[]{:S(2)}) collective-permute-start(bf16[2,20,2,128]{3,1,2,0:T(8,128)(2,1)S(1)} %get-tuple-element.149), channel_id=1, source_target_pairs={{0,1},{1,2},{2,3},{3,0},{4,5},{5,6},{6,7},{7,4},{8,9},{9,10},{10,1... | collective-permute-start | bytes 61448 | tf_op jit(solution)/shard_map/while/body/eval_jaxpr/ppermute | solution.py:16
  128.4 3.3 %collective-permute-start.1 = (bf16[2,20,2,128]{3,1,2,0:T(8,128)(2,1)S(1)}, bf16[2,20,2,128]{3,1,2,0:T(8,128)(2,1)S(1)}, u32[]{:S(2)}, u32[]{:S(2)}) collective-permute-start(bf16[2,20,2,128]{3,1,2,0:T(8,128)(2,1)S(1)} %get-tuple-element.149), channel_id=1, source_target_pairs={{0,1},{1,2},{2,3},{3,0},{4,5},{5,6},{6,7},{7,4},{8,9},{9,10},{10,1... | collective-permute-start | bytes 61448 | tf_op jit(solution)/shard_map/while/body/eval_jaxpr/ppermute | solution.py:16
  138.9 3.3 %collective-permute-start.1 = (bf16[2,20,2,128]{3,1,2,0:T(8,128)(2,1)S(1)}, bf16[2,20,2,128]{3,1,2,0:T(8,128)(2,1)S(1)}, u32[]{:S(2)}, u32[]{:S(2)}) collective-permute-start(bf16[2,20,2,128]{3,1,2,0:T(8,128)(2,1)S(1)} %get-tuple-element.149), channel_id=1, source_target_pairs={{0,1},{1,2},{2,3},{3,0},{4,5},{5,6},{6,7},{7,4},{8,9},{9,10},{10,1... | collective-permute-start | bytes 61448 | tf_op jit(solution)/shard_map/while/body/eval_jaxpr/ppermute | solution.py:16
  149.4 3.3 %collective-permute-start.1 = (bf16[2,20,2,128]{3,1,2,0:T(8,128)(2,1)S(1)}, bf16[2,20,2,128]{3,1,2,0:T(8,128)(2,1)S(1)}, u32[]{:S(2)}, u32[]{:S(2)}) collective-permute-start(bf16[2,20,2,128]{3,1,2,0:T(8,128)(2,1)S(1)} %get-tuple-element.149), channel_id=1, source_target_pairs={{0,1},{1,2},{2,3},{3,0},{4,5},{5,6},{6,7},{7,4},{8,9},{9,10},{10,1... | collective-permute-start | bytes 61448 | tf_op jit(solution)/shard_map/while/body/eval_jaxpr/ppermute | solution.py:16
  160.0 3.3 %collective-permute-start.1 = (bf16[2,20,2,128]{3,1,2,0:T(8,128)(2,1)S(1)}, bf16[2,20,2,128]{3,1,2,0:T(8,128)(2,1)S(1)}, u32[]{:S(2)}, u32[]{:S(2)}) collective-permute-start(bf16[2,20,2,128]{3,1,2,0:T(8,128)(2,1)S(1)} %get-tuple-element.149), channel_id=1, source_target_pairs={{0,1},{1,2},{2,3},{3,0},{4,5},{5,6},{6,7},{7,4},{8,9},{9,10},{10,1... | collective-permute-start | bytes 61448 | tf_op jit(solution)/shard_map/while/body/eval_jaxpr/ppermute | solution.py:16
  170.5 3.3 %collective-permute-start.1 = (bf16[2,20,2,128]{3,1,2,0:T(8,128)(2,1)S(1)}, bf16[2,20,2,128]{3,1,2,0:T(8,128)(2,1)S(1)}, u32[]{:S(2)}, u32[]{:S(2)}) collective-permute-start(bf16[2,20,2,128]{3,1,2,0:T(8,128)(2,1)S(1)} %get-tuple-element.149), channel_id=1, source_target_pairs={{0,1},{1,2},{2,3},{3,0},{4,5},{5,6},{6,7},{7,4},{8,9},{9,10},{10,1... | collective-permute-start | bytes 61448 | tf_op jit(solution)/shard_map/while/body/eval_jaxpr/ppermute | solution.py:16
  181.1 3.3 %collective-permute-start.1 = (bf16[2,20,2,128]{3,1,2,0:T(8,128)(2,1)S(1)}, bf16[2,20,2,128]{3,1,2,0:T(8,128)(2,1)S(1)}, u32[]{:S(2)}, u32[]{:S(2)}) collective-permute-start(bf16[2,20,2,128]{3,1,2,0:T(8,128)(2,1)S(1)} %get-tuple-element.149), channel_id=1, source_target_pairs={{0,1},{1,2},{2,3},{3,0},{4,5},{5,6},{6,7},{7,4},{8,9},{9,10},{10,1... | collective-permute-start | bytes 61448 | tf_op jit(solution)/shard_map/while/body/eval_jaxpr/ppermute | solution.py:16
  191.6 3.3 %collective-permute-start.1 = (bf16[2,20,2,128]{3,1,2,0:T(8,128)(2,1)S(1)}, bf16[2,20,2,128]{3,1,2,0:T(8,128)(2,1)S(1)}, u32[]{:S(2)}, u32[]{:S(2)}) collective-permute-start(bf16[2,20,2,128]{3,1,2,0:T(8,128)(2,1)S(1)} %get-tuple-element.149), channel_id=1, source_target_pairs={{0,1},{1,2},{2,3},{3,0},{4,5},{5,6},{6,7},{7,4},{8,9},{9,10},{10,1... | collective-permute-start | bytes 61448 | tf_op jit(solution)/shard_map/while/body/eval_jaxpr/ppermute | solution.py:16
  (14 other events, 221.8 us)
where the time goes:
time: 272 us; the launch traced here: 270 us
  matrix products  109 us (40%)
  blocking collectives  59.6 us (22%)
  waiting for transfers between devices  50.7 us (19%)
  local copies, waits for them, and re-layouts  26.8 us (10%)
  starting transfers between devices  15.2 us (6%)
  other arithmetic  6.83 us (3%)
    dot_general x18, matrix products, transport(): jnp.einsum('srkpq,strkq->strp', tiles_part, picked, preferred_element_typ...  85.2 us
    ppermute x18, waiting for transfers between devices, with_halo(): lax.ppermute(tail, axis, [(i, (i + 1) % count) for i in range(count)])  32.2 us
    psum x1, blocking collectives, on_device(): squared = lax.psum(jnp.sum(orthogonal * orthogonal), ('seg', 'blk'))  30.1 us
    psum x1, blocking collectives, on_device(): proj = lax.psum(local_proj, ('seg', 'blk'))  29.5 us
    gather x18, local copies, waits for them, and re-layouts, pick_blocks(): return jnp.take(whole, cols_s.reshape(-1), axis=1)  23.9 us
    dot_general x18, matrix products, forcing(): jnp.einsum('tu,sunp->stnp', coupling, slope * u, precision=lax.Precision....  18.7 us
    ppermute x18, waiting for transfers between devices, with_halo(): lax.ppermute(head, axis, [((i + 1) % count, i) for i in range(count)])  18.5 us
    ppermute x18, starting transfers between devices, with_halo(): lax.ppermute(tail, axis, [(i, (i + 1) % count) for i in range(count)])  8.45 us
  transfers between devices with their start and end apart: 37, of which 36 were waited for; matrix products, arithmetic and copies ran while one was open for 49% of the time, Pallas kernels for 0%

commit v1 on v0

v1 whole, which is shorter than its diff:
```python
import functools

import jax
import jax.numpy as jnp
from jax import lax
from jax.experimental import pallas as pl
from jax.experimental.pallas import tpu as pltpu
from jax.sharding import PartitionSpec as P

STEPS = 18
MESH = pl.DeviceIdType.MESH
REACH = 2
PAD = 32


def merge_kernel(total, rows, stored, cols_ref, tiles_ref, w_ref, acc):
    s, g = pl.program_id(0), pl.program_id(1)
    first = lax.axis_index("blk") * rows
    acc[...] = jnp.zeros_like(acc)
    wide = 2 * REACH + 2
    for j in range(2):
        row = 2 * g + j

        def add(k, unused):
            col = cols_ref[(s * rows + row) * stored + k]
            d = lax.rem(col - first - row + (REACH + total), total)
            at = j * wide + j + d
            acc[at] += tiles_ref[0, j, k].astype(jnp.float32)
            return unused

        lax.fori_loop(0, stored, add, 0, unroll=2)
    size = acc.shape[1]
    for j in range(2):
        for c in range(wide):
            w_ref[0, 0, j * size:(j + 1) * size, c * size:(c + 1) * size] = (
                acc[j * wide + c].astype(jnp.bfloat16)
            )


def steps_kernel(
    dims, base_ref, dir_ref, coup_ref, wet_ref, w_hbm, basis_hbm, orth_ref, coef_ref,
    w, basis, drive, slope, cc, wetf, follow, native, part1, part2,
    send_sem, recv_sem, follow_sem, load_sem, red_sem1, red_sem2,
):
    segs, tracers, rows, points, kry, n_seg, n_blk, entries = dims
    pairs = rows // 2
    per = tracers * rows
    me_seg, me_blk = lax.axis_index("seg"), lax.axis_index("blk")
    left, right = lax.rem(me_blk + n_blk - 1, n_blk), lax.rem(me_blk + 1, n_blk)

    w_copy = pltpu.make_async_copy(w_hbm, w, load_sem.at[0])
    basis_copy = pltpu.make_async_copy(basis_hbm, basis, load_sem.at[1])
    w_copy.start()
    basis_copy.start()

    barrier = pltpu.get_barrier_semaphore()
    for i in range(1, n_blk):
        pl.semaphore_signal(barrier, inc=1, device_id={"blk": lax.rem(me_blk + i, n_blk)}, device_id_type=MESH)
    for i in range(1, n_seg):
        pl.semaphore_signal(barrier, inc=1, device_id={"seg": lax.rem(me_seg + i, n_seg)}, device_id_type=MESH)

    c = 0.5 * coup_ref[...]
    high = c.astype(jnp.bfloat16)
    low = (c - high.astype(jnp.float32)).astype(jnp.bfloat16)
    cc[...] = jnp.zeros_like(cc)
    cc[:tracers, 0:tracers] = high.astype(jnp.float32)
    cc[:tracers, PAD:PAD + tracers] = high.astype(jnp.float32)
    cc[:tracers, 2 * PAD:2 * PAD + tracers] = low.astype(jnp.float32)
    mix = cc[...].astype(jnp.bfloat16)
    slope[...] = jnp.zeros_like(slope)
    native[...] = jnp.zeros_like(native)
    for r in range(rows):
        lanes = slice(r * points, (r + 1) * points)
        wetf[:, lanes] = wet_ref[r:r + 1, :].astype(jnp.float32)
        for s in range(segs):
            t = jnp.tanh(base_ref[pl.ds(s * per + r, tracers, stride=rows), :])
            slope[s, :tracers, lanes] = 1.0 - t * t
            native[s, :tracers, lanes] = dir_ref[pl.ds(s * per + r, tracers, stride=rows), :]

    def lanes_of(g, blocks=2):
        return slice(2 * g * points, (2 * g + blocks) * points)

    def force(u, s, g, slot):
        x = slope[s, :, lanes_of(g)] * u
        xh = x.astype(jnp.bfloat16)
        xl = (x - xh.astype(jnp.float32)).astype(jnp.bfloat16)
        stack = jnp.concatenate([xh, xl, xh], axis=0)
        d = u + jnp.dot(mix, stack, preferred_element_type=jnp.float32)
        drive[slot, s, :, lanes_of(g + 1)] = d.astype(jnp.bfloat16)

    def move(s, g, slot):
        m = lax.dot_general(
            drive[slot, s, :, lanes_of(g, 2 * REACH + 2)], w[s, g],
            (((1,), (1,)), ((), ())), preferred_element_type=jnp.float32,
        )
        return m * wetf[:, lanes_of(g)]

    def halos(s, slot):
        return [
            pltpu.make_async_remote_copy(
                src_ref=drive.at[slot, s, :, lanes_of(1)],
                dst_ref=drive.at[slot, s, :, lanes_of(pairs + 1)],
                send_sem=send_sem.at[slot, s, 0], recv_sem=recv_sem.at[slot, s, 0],
                device_id={"blk": left}, device_id_type=MESH,
            ),
            pltpu.make_async_remote_copy(
                src_ref=drive.at[slot, s, :, lanes_of(pairs)],
                dst_ref=drive.at[slot, s, :, lanes_of(0)],
                send_sem=send_sem.at[slot, s, 1], recv_sem=recv_sem.at[slot, s, 1],
                device_id={"blk": right}, device_id_type=MESH,
            ),
        ]

    edges, inner = (0, pairs - 1), range(1, pairs - 1)
    for s in range(segs):
        for g in edges:
            force(native[s, :, lanes_of(g)], s, g, 0)
    pl.semaphore_wait(barrier, n_blk + n_seg - 2)
    for s in range(segs):
        for h in halos(s, 0):
            h.start()
    follow_copy = pltpu.make_async_remote_copy(
        src_ref=dir_ref.at[0:per], dst_ref=follow, send_sem=follow_sem.at[0], recv_sem=follow_sem.at[1],
        device_id={"seg": lax.rem(me_seg + n_seg - 1, n_seg)}, device_id_type=MESH,
    )
    follow_copy.start()
    for s in range(segs):
        for g in inner:
            force(native[s, :, lanes_of(g)], s, g, 0)

    basis_copy.wait()
    chunks = segs * tracers
    half = kry // 2 + 1

    def fold(a):
        return jnp.sum(a, axis=0, keepdims=True)

    def gram(i, acc):
        b = [basis[j, pl.ds(pl.multiple_of(i * rows, rows), rows), :] for j in range(kry)]
        return tuple(acc[m * kry + j] + b[j] * b[(j + m) % kry] for m in range(half) for j in range(kry))

    zero = jnp.zeros((rows, points), jnp.float32)
    sums = lax.fori_loop(0, chunks, gram, (zero,) * (half * kry))
    for m in range(half):
        for j in range(kry):
            part1[me_blk, pl.ds((m + 2) * 8 + j, 1), :] = fold(sums[m * kry + j])

    w_copy.wait()

    def step(slot):
        for s in range(segs):
            for h in halos(s, slot):
                h.wait()
            for g in edges:
                force(move(s, g, slot), s, g, 1 - slot)
            for h in halos(s, 1 - slot):
                h.start()
        for s in range(segs):
            for g in inner:
                force(move(s, g, slot), s, g, 1 - slot)

    def two(i, unused):
        step(0)
        step(1)
        return unused

    lax.fori_loop(0, (STEPS - 1) // 2, two, 0)
    for n in range((STEPS - 1) // 2 * 2, STEPS - 1):
        step(n % 2)
    last = (STEPS - 1) % 2
    for s in range(segs):
        for g in inner:
            native[s, :, lanes_of(g)] = move(s, g, last)
    for s in range(segs):
        for h in halos(s, last):
            h.wait()
        for g in edges:
            native[s, :, lanes_of(g)] = move(s, g, last)
    for s in range(segs):
        for r in range(rows):
            orth_ref[pl.ds(s * per + r, tracers, stride=rows), :] = native[s, :tracers, r * points:(r + 1) * points]
    follow_copy.wait()

    def project(i, acc):
        here = pl.ds(pl.multiple_of(i * rows, rows), rows)
        there = pl.ds(pl.multiple_of(i * rows, rows) + per, rows)
        far = pl.ds(pl.multiple_of(i * rows, rows) + (segs - 1) * per, rows)
        for s in range(segs):
            at = pl.ds(pl.multiple_of(i * rows, rows) + s * per, rows)
            if s < segs - 1:
                nxt = dir_ref[pl.ds(pl.multiple_of(i * rows, rows) + (s + 1) * per, rows), :]
            else:
                nxt = follow[here, :]
            shot = orth_ref[at, :] - nxt
            orth_ref[at, :] = shot
            acc = tuple(acc[j] + basis[j, at, :] * shot for j in range(kry)) + (acc[kry] + shot * shot,)
        return acc

    sums = lax.fori_loop(0, tracers, project, (zero,) * (kry + 1), unroll=4)
    for j in range(kry):
        part1[me_blk, pl.ds(j, 1), :] = fold(sums[j])
    part1[me_blk, pl.ds(8, 8), :] = sums[kry]

    def everyone(part, me, axis, count, sems):
        copies = [
            pltpu.make_async_remote_copy(
                src_ref=part.at[me], dst_ref=part.at[me],
                send_sem=sems.at[0, i - 1], recv_sem=sems.at[1, i - 1],
                device_id={axis: lax.rem(me + i, count)}, device_id_type=MESH,
            )
            for i in range(1, count)
        ]
        for x in copies:
            x.start()
        for x in copies:
            x.wait()
        result = part[0]
        for i in range(1, count):
            result = result + part[i]
        return result

    part2[me_seg] = everyone(part1, me_blk, "blk", n_blk, red_sem1)
    both = everyone(part2, me_seg, "seg", n_seg, red_sem2)
    sumd = jnp.sum(both, axis=1, keepdims=True)
    h = sumd[0:kry]
    hv = [sumd[j:j + 1] for j in range(kry)]
    quad = jnp.zeros((kry, 1), jnp.float32)
    for m in range(half):
        turned = h if m == 0 else jnp.concatenate([h[m:], h[:m]], axis=0)
        weight = 1.0 if m == 0 or 2 * m == kry else 2.0
        quad = quad + weight * (turned * sumd[(m + 2) * 8:(m + 2) * 8 + kry])
    quad = h * (quad - 2.0 * h) + sumd[8:16]
    square = jnp.sum(jnp.broadcast_to(quad, (kry, points)), axis=0, keepdims=True)
    length = jnp.sqrt(jnp.maximum(square, 0.0) / entries)
    coef_ref[kry] = length[0, 0]
    for j in range(kry):
        coef_ref[j] = hv[j][0, 0]
    wide = [jnp.broadcast_to(x, (rows, points)) for x in hv]

    def subtract(i, unused):
        at = pl.ds(pl.multiple_of(i * rows, rows), rows)
        a = hv_sum([wide[j] * basis[j, at, :] for j in range(kry)])
        orth_ref[at, :] = orth_ref[at, :] - a
        return unused

    lax.fori_loop(0, chunks, subtract, 0, unroll=4)


def hv_sum(terms):
    while len(terms) > 1:
        terms = [sum(terms[i:i + 2]) for i in range(0, len(terms), 2)]
    return terms[0]


def on_device(n_seg, n_blk, base_state, direction, coupling, tiles, columns, wet, basis):
    segs, tracers, rows, points = direction.shape
    stored = tiles.shape[2]
    kry = basis.shape[0]
    total = rows * n_blk
    entries = float(segs * n_seg * tracers * total * points)
    pairs = rows // 2
    wide = 2 * REACH + 2
    w = pl.pallas_call(
        functools.partial(merge_kernel, total, rows, stored),
        out_shape=jax.ShapeDtypeStruct((segs, pairs, 2 * points, wide * points), jnp.bfloat16),
        grid_spec=pltpu.PrefetchScalarGridSpec(
            num_scalar_prefetch=1,
            grid=(segs, pairs),
            in_specs=[pl.BlockSpec((1, 2, stored, points, points), lambda s, g, c: (s, g, 0, 0, 0))],
            out_specs=pl.BlockSpec((1, 1, 2 * points, wide * points), lambda s, g, c: (s, g, 0, 0)),
            scratch_shapes=[pltpu.VMEM((2 * wide, points, points), jnp.float32)],
        ),
        compiler_params=pltpu.CompilerParams(vmem_limit_bytes=24 << 20),
        name="merge",
    )(columns.reshape(-1), tiles)
    flat = segs * tracers * rows
    dims = (segs, tracers, rows, points, kry, n_seg, n_blk, entries)
    in_vmem = pl.BlockSpec(memory_space=pltpu.VMEM)
    anywhere = pl.BlockSpec(memory_space=pl.ANY)
    red = (2 + kry // 2 + 1) * 8
    orth, coef = pl.pallas_call(
        functools.partial(steps_kernel, dims),
        out_shape=(
            jax.ShapeDtypeStruct((flat, points), jnp.float32),
            jax.ShapeDtypeStruct((kry + 1,), jnp.float32),
        ),
        in_specs=[in_vmem] * 4 + [anywhere] * 2,
        out_specs=(in_vmem, pl.BlockSpec(memory_space=pltpu.SMEM)),
        scratch_shapes=[
            pltpu.VMEM((segs, pairs, 2 * points, wide * points), jnp.bfloat16),
            pltpu.VMEM((kry, flat, points), jnp.float32),
            pltpu.VMEM((2, segs, PAD, (rows + 2 * REACH) * points), jnp.bfloat16),
            pltpu.VMEM((segs, PAD, rows * points), jnp.float32),
            pltpu.VMEM((PAD, 3 * PAD), jnp.float32),
            pltpu.VMEM((1, rows * points), jnp.float32),
            pltpu.VMEM((tracers * rows, points), jnp.float32),
            pltpu.VMEM((segs, PAD, rows * points), jnp.float32),
            pltpu.VMEM((n_blk, red, points), jnp.float32),
            pltpu.VMEM((n_seg, red, points), jnp.float32),
            pltpu.SemaphoreType.DMA((2, segs, 2)),
            pltpu.SemaphoreType.DMA((2, segs, 2)),
            pltpu.SemaphoreType.DMA((2,)),
            pltpu.SemaphoreType.DMA((2,)),
            pltpu.SemaphoreType.DMA((2, n_blk - 1)),
            pltpu.SemaphoreType.DMA((2, n_seg - 1)),
        ],
        compiler_params=pltpu.CompilerParams(
            collective_id=0, has_side_effects=True, vmem_limit_bytes=40 << 20
        ),
        name="steps",
    )(
        base_state.reshape(flat, points), direction.reshape(flat, points), coupling, wet,
        w, basis.reshape(kry, flat, points),
    )
    return orth.reshape(direction.shape), coef


def solution(mesh):
    in_specs = (
        P(("groups", "seg"), None, "blk", None),
        P(("groups", "seg"), None, "blk", None),
        P("groups", None),
        P("seg", "blk", None, None, None),
        P("seg", "blk", None),
        P("blk", None),
        P(None, ("groups", "seg"), None, "blk", None),
    )
    out_specs = (P(("groups", "seg"), None, "blk", None), P("groups"))
    body = functools.partial(on_device, mesh.shape["seg"], mesh.shape["blk"])
    return jax.shard_map(body, mesh=mesh, in_specs=in_specs, out_specs=out_specs, check_vma=False)
```

time: 272 us -> 81.2 us (0.30)
  matrix products: 109 us -> 0 us
  Pallas kernels: 0 us -> 74.9 us
  blocking collectives: 59.6 us -> 0 us
  waiting for transfers between devices: 50.7 us -> 0 us
  local copies, waits for them, and re-layouts: 26.8 us -> 5.36 us
  starting transfers between devices: 15.2 us -> 0 us
  other arithmetic: 6.83 us -> 0 us
    dot_general x38 -> x0, matrix products: 109 us -> none  [the longest x18 85.2 us: transport(): jnp.einsum('srkpq,strkq->strp', tiles_part, picked, preferred_element_typ...]
    pallas_call x0 -> x2, Pallas kernels: none -> 74.9 us  [the longest x1 70.5 us: on_device(): pl.pallas_call(functools.partial(steps_kernel, dims), out_shape=(jax.Shap...]
    psum x2 -> x0, blocking collectives: 59.6 us -> none  [the longest x1 30.1 us: on_device(): squared = lax.psum(jnp.sum(orthogonal * orthogonal), ('seg', 'blk'))]
    ppermute x37 -> x0, waiting for transfers between devices: 50.7 us -> none  [the longest x18 32.2 us: with_halo(): lax.ppermute(tail, axis, [(i, (i + 1) % count) for i in range(count)])]
    gather x18 -> x0, local copies, waits for them, and re-layouts: 23.9 us -> none  [pick_blocks(): return jnp.take(whole, cols_s.reshape(-1), axis=1)]
    ppermute x37 -> x0, starting transfers between devices: 15.2 us -> none  [the longest x18 8.45 us: with_halo(): lax.ppermute(tail, axis, [(i, (i + 1) % count) for i in range(count)])]
    unnamed x2 -> x14, local copies, waits for them, and re-layouts: 0.01 us -> 4.59 us
  transfers between devices with their start and end apart: 37 -> 0, of which waited for: 36 -> 0; matrix products, arithmetic and copies ran while one was open for 49% -> 0% of each run, Pallas kernels for 0% -> 0%
where the time goes in v1:
time: 81.2 us; the launch traced here: 81 us
  Pallas kernels  74.9 us (92%)
  local copies, waits for them, and re-layouts  5.36 us (7%)
    pallas_call x1, Pallas kernels, on_device(): pl.pallas_call(functools.partial(steps_kernel, dims), out_shape=(jax.Shap...  70.5 us
    unnamed x14, local copies, waits for them, and re-layouts  4.59 us
    pallas_call x1, Pallas kernels, on_device(): pl.pallas_call(functools.partial(merge_kernel, total, rows, stored), out_...  4.41 us

profile of v1, /device:TPU:0, one launch (start us, length us, event | category | flops | bytes accessed | tf_op | source)
XLA Modules:
  0.0 81.0 jit_solution(12792267229424459450)
XLA Ops:
  0.6 0.8 reshape.21.cols_ref
  1.4 0.0 copy-start
  1.4 3.4 %copy-done = bf16[2,8,16,128,128]{4,3,2,1,0:T(8,128)(2,1)S(1)} copy-done((bf16[2,8,16,128,128]{4,3,2,1,0:T(8,128)(2,1)S(1)}, bf16[2,8,16,128,128]{4,3,2,1,0:T(8,128)(2,1)}, u32[]{:S(2)}) %copy-start) | copy-done | bytes 8388632
  4.8 0.0 copy-start.1
  4.8 0.0 copy-start.2
  4.8 0.0 copy-start.3
  4.8 0.0 copy-start.4
  4.8 0.0 copy-start.5
  4.8 4.4 %merge.1.w_hbm = bf16[2,4,256,768]{3,2,1,0:T(8,128)(2,1)S(1)} custom-call(s32[256]{0:T(256)S(1)} %reshape.21.cols_ref, bf16[2,8,16,128,128]{4,3,2,1,0:T(8,128)(2,1)S(1)} %copy-done), custom_call_target="tpu_custom_call" | custom-call | tf_op jit(solution)/shard_map/merge/pallas_call | solution.py:263
  9.2 0.0 copy-done.1
  9.2 0.0 copy-done.2
  9.3 0.0 copy-done.3
  9.3 0.0 copy-done.4
  9.3 0.0 copy-done.5
  9.3 70.5 %steps.1 = (f32[320,128]{1,0:T(8,128)S(1)}, f32[9]{0:T(128)S(1)}) custom-call(f32[320,128]{1,0:T(8,128)S(1)} %bitcast.5, f32[320,128]{1,0:T(8,128)S(1)} %bitcast.6, f32[20,20]{1,0:T(8,128)S(1)} %copy-done.4, s32[8,128]{1,0:T(8,128)S(1)} %copy-done.5, bf16[2,4,256,768]{3,2,1,0:T(8,128)(2,1)S(1)} %merge.1.w_hbm, f32[8,320,128]{2,1,0:T(8,128)S(1)} %bitcast.4), custom_call_target="tpu_custom_call" | custom-call | tf_op jit(solution)/shard_map/steps/pallas_call | solution.py:281
  79.8 0.7 copy.11
  80.4 0.5 copy.12
Async XLA Ops:
  1.4 3.4 %copy-start = (bf16[2,8,16,128,128]{4,3,2,1,0:T(8,128)(2,1)S(1)}, bf16[2,8,16,128,128]{4,3,2,1,0:T(8,128)(2,1)}, u32[]{:S(2)}) copy-start(bf16[2,8,16,128,128]{4,3,2,1,0:T(8,128)(2,1)} %tiles_ref.1) | copy-start | bytes 25165828
  4.8 4.4 %copy-start.1 = (f32[8,2,20,8,128]{4,3,2,1,0:T(8,128)S(1)}, f32[8,2,20,8,128]{4,3,2,1,0:T(8,128)}, u32[]{:S(2)}) copy-start(f32[8,2,20,8,128]{4,3,2,1,0:T(8,128)} %param.13) | copy-start | bytes 3932164
  4.8 4.4 %copy-start.2 = (f32[2,20,8,128]{3,2,1,0:T(8,128)S(1)}, f32[2,20,8,128]{3,2,1,0:T(8,128)}, u32[]{:S(2)}) copy-start(f32[2,20,8,128]{3,2,1,0:T(8,128)} %param.7) | copy-start | bytes 491524
  4.8 4.5 %copy-start.3 = (f32[2,20,8,128]{3,2,1,0:T(8,128)S(1)}, f32[2,20,8,128]{3,2,1,0:T(8,128)}, u32[]{:S(2)}) copy-start(f32[2,20,8,128]{3,2,1,0:T(8,128)} %param.8) | copy-start | bytes 491524
  4.8 4.5 %copy-start.4 = (f32[20,20]{1,0:T(8,128)S(1)}, f32[20,20]{1,0:T(8,128)}, u32[]{:S(2)}) copy-start(f32[20,20]{1,0:T(8,128)} %coup_ref.1) | copy-start | bytes 4804
  4.8 4.5 %copy-start.5 = (s32[8,128]{1,0:T(8,128)S(1)}, s32[8,128]{1,0:T(8,128)}, u32[]{:S(2)}) copy-start(s32[8,128]{1,0:T(8,128)} %wet_ref.1) | copy-start | bytes 12292

commit v2 on v1

--- a/solution.py
+++ b/solution.py
@@ -32,8 +32,8 @@
     size = acc.shape[1]
     for j in range(2):
         for c in range(wide):
-            w_ref[0, 0, j * size:(j + 1) * size, c * size:(c + 1) * size] = (
-                acc[j * wide + c].astype(jnp.bfloat16)
+            w_ref[0, 0, c * size:(c + 1) * size, j * size:(j + 1) * size] = (
+                acc[j * wide + c].T.astype(jnp.bfloat16)
             )
 
 
@@ -64,8 +64,7 @@
     low = (c - high.astype(jnp.float32)).astype(jnp.bfloat16)
     cc[...] = jnp.zeros_like(cc)
     cc[:tracers, 0:tracers] = high.astype(jnp.float32)
-    cc[:tracers, PAD:PAD + tracers] = high.astype(jnp.float32)
-    cc[:tracers, 2 * PAD:2 * PAD + tracers] = low.astype(jnp.float32)
+    cc[:tracers, PAD:PAD + tracers] = low.astype(jnp.float32)
     mix = cc[...].astype(jnp.bfloat16)
     slope[...] = jnp.zeros_like(slope)
     native[...] = jnp.zeros_like(native)
@@ -83,15 +82,14 @@
     def force(u, s, g, slot):
         x = slope[s, :, lanes_of(g)] * u
         xh = x.astype(jnp.bfloat16)
-        xl = (x - xh.astype(jnp.float32)).astype(jnp.bfloat16)
-        stack = jnp.concatenate([xh, xl, xh], axis=0)
+        stack = jnp.concatenate([xh, xh], axis=0)
         d = u + jnp.dot(mix, stack, preferred_element_type=jnp.float32)
         drive[slot, s, :, lanes_of(g + 1)] = d.astype(jnp.bfloat16)
 
     def move(s, g, slot):
-        m = lax.dot_general(
+        m = jnp.dot(
             drive[slot, s, :, lanes_of(g, 2 * REACH + 2)], w[s, g],
-            (((1,), (1,)), ((), ())), preferred_element_type=jnp.float32,
+            preferred_element_type=jnp.float32,
         )
         return m * wetf[:, lanes_of(g)]
 
@@ -262,12 +260,12 @@
     wide = 2 * REACH + 2
     w = pl.pallas_call(
         functools.partial(merge_kernel, total, rows, stored),
-        out_shape=jax.ShapeDtypeStruct((segs, pairs, 2 * points, wide * points), jnp.bfloat16),
+        out_shape=jax.ShapeDtypeStruct((segs, pairs, wide * points, 2 * points), jnp.bfloat16),
         grid_spec=pltpu.PrefetchScalarGridSpec(
             num_scalar_prefetch=1,
             grid=(segs, pairs),
             in_specs=[pl.BlockSpec((1, 2, stored, points, points), lambda s, g, c: (s, g, 0, 0, 0))],
-            out_specs=pl.BlockSpec((1, 1, 2 * points, wide * points), lambda s, g, c: (s, g, 0, 0)),
+            out_specs=pl.BlockSpec((1, 1, wide * points, 2 * points), lambda s, g, c: (s, g, 0, 0)),
             scratch_shapes=[pltpu.VMEM((2 * wide, points, points), jnp.float32)],
         ),
         compiler_params=pltpu.CompilerParams(vmem_limit_bytes=24 << 20),
@@ -287,11 +285,11 @@
         in_specs=[in_vmem] * 4 + [anywhere] * 2,
         out_specs=(in_vmem, pl.BlockSpec(memory_space=pltpu.SMEM)),
         scratch_shapes=[
-            pltpu.VMEM((segs, pairs, 2 * points, wide * points), jnp.bfloat16),
+            pltpu.VMEM((segs, pairs, wide * points, 2 * points), jnp.bfloat16),
             pltpu.VMEM((kry, flat, points), jnp.float32),
             pltpu.VMEM((2, segs, PAD, (rows + 2 * REACH) * points), jnp.bfloat16),
             pltpu.VMEM((segs, PAD, rows * points), jnp.float32),
-            pltpu.VMEM((PAD, 3 * PAD), jnp.float32),
+            pltpu.VMEM((PAD, 2 * PAD), jnp.float32),
             pltpu.VMEM((1, rows * points), jnp.float32),
             pltpu.VMEM((tracers * rows, points), jnp.float32),
             pltpu.VMEM((segs, PAD, rows * points), jnp.float32),

time: 81.2 us -> 79.4 us (0.978)
  Pallas kernels: 74.9 us -> 73.2 us
    pallas_call x1, Pallas kernels: 70.5 us -> 67.8 us  [on_device(): pl.pallas_call(functools.partial(steps_kernel, dims), out_shape=(jax.Shap...]
    pallas_call x1, Pallas kernels: 4.41 us -> 5.34 us  [on_device(): pl.pallas_call(functools.partial(merge_kernel, total, rows, stored), out_...]
where the time goes in v2:
time: 79.4 us; the launch traced here: 79.2 us
  Pallas kernels  73.2 us (92%)
  local copies, waits for them, and re-layouts  5.36 us (7%)
    pallas_call x1, Pallas kernels, on_device(): pl.pallas_call(functools.partial(steps_kernel, dims), out_shape=(jax.Shap...  67.8 us
    pallas_call x1, Pallas kernels, on_device(): pl.pallas_call(functools.partial(merge_kernel, total, rows, stored), out_...  5.34 us
    unnamed x14, local copies, waits for them, and re-layouts  4.59 us

profile of v2, /device:TPU:0, one launch (start us, length us, event | category | flops | bytes accessed | tf_op | source)
XLA Modules:
  0.0 79.2 jit_solution(3984180109855611621)
XLA Ops:
  0.6 0.8 reshape.21.cols_ref
  1.4 0.0 copy-start
  1.4 3.4 %copy-done = bf16[2,8,16,128,128]{4,3,2,1,0:T(8,128)(2,1)S(1)} copy-done((bf16[2,8,16,128,128]{4,3,2,1,0:T(8,128)(2,1)S(1)}, bf16[2,8,16,128,128]{4,3,2,1,0:T(8,128)(2,1)}, u32[]{:S(2)}) %copy-start) | copy-done | bytes 8388632
  4.8 0.0 copy-start.1
  4.8 0.0 copy-start.2
  4.8 0.0 copy-start.3
  4.8 0.0 copy-start.4
  4.8 0.0 copy-start.5
  4.8 5.3 %merge.1.w_hbm = bf16[2,4,768,256]{3,2,1,0:T(8,128)(2,1)S(1)} custom-call(s32[256]{0:T(256)S(1)} %reshape.21.cols_ref, bf16[2,8,16,128,128]{4,3,2,1,0:T(8,128)(2,1)S(1)} %copy-done), custom_call_target="tpu_custom_call" | custom-call | tf_op jit(solution)/shard_map/merge/pallas_call | solution.py:261
  10.2 0.0 copy-done.1
  10.2 0.0 copy-done.2
  10.2 0.0 copy-done.3
  10.2 0.0 copy-done.4
  10.2 0.0 copy-done.5
  10.2 67.8 %steps.1 = (f32[320,128]{1,0:T(8,128)S(1)}, f32[9]{0:T(128)S(1)}) custom-call(f32[320,128]{1,0:T(8,128)S(1)} %bitcast.5, f32[320,128]{1,0:T(8,128)S(1)} %bitcast.6, f32[20,20]{1,0:T(8,128)S(1)} %copy-done.4, s32[8,128]{1,0:T(8,128)S(1)} %copy-done.5, bf16[2,4,768,256]{3,2,1,0:T(8,128)(2,1)S(1)} %merge.1.w_hbm, f32[8,320,128]{2,1,0:T(8,128)S(1)} %bitcast.4), custom_call_target="tpu_custom_call" | custom-call | tf_op jit(solution)/shard_map/steps/pallas_call | solution.py:279
  78.0 0.7 copy.11
  78.7 0.5 copy.12
Async XLA Ops:
  1.4 3.4 %copy-start = (bf16[2,8,16,128,128]{4,3,2,1,0:T(8,128)(2,1)S(1)}, bf16[2,8,16,128,128]{4,3,2,1,0:T(8,128)(2,1)}, u32[]{:S(2)}) copy-start(bf16[2,8,16,128,128]{4,3,2,1,0:T(8,128)(2,1)} %tiles_ref.1) | copy-start | bytes 25165828
  4.8 5.4 %copy-start.1 = (f32[8,2,20,8,128]{4,3,2,1,0:T(8,128)S(1)}, f32[8,2,20,8,128]{4,3,2,1,0:T(8,128)}, u32[]{:S(2)}) copy-start(f32[8,2,20,8,128]{4,3,2,1,0:T(8,128)} %param.13) | copy-start | bytes 3932164
  4.8 5.4 %copy-start.2 = (f32[2,20,8,128]{3,2,1,0:T(8,128)S(1)}, f32[2,20,8,128]{3,2,1,0:T(8,128)}, u32[]{:S(2)}) copy-start(f32[2,20,8,128]{3,2,1,0:T(8,128)} %param.7) | copy-start | bytes 491524
  4.8 5.4 %copy-start.3 = (f32[2,20,8,128]{3,2,1,0:T(8,128)S(1)}, f32[2,20,8,128]{3,2,1,0:T(8,128)}, u32[]{:S(2)}) copy-start(f32[2,20,8,128]{3,2,1,0:T(8,128)} %param.8) | copy-start | bytes 491524
  4.8 5.4 %copy-start.4 = (f32[20,20]{1,0:T(8,128)S(1)}, f32[20,20]{1,0:T(8,128)}, u32[]{:S(2)}) copy-start(f32[20,20]{1,0:T(8,128)} %coup_ref.1) | copy-start | bytes 4804
  4.8 5.4 %copy-start.5 = (s32[8,128]{1,0:T(8,128)S(1)}, s32[8,128]{1,0:T(8,128)}, u32[]{:S(2)}) copy-start(s32[8,128]{1,0:T(8,128)} %wet_ref.1) | copy-start | bytes 12292
